TPU v7x, 128 devices: a whole 4x4x4 slice. The times are simulated.
128 devices in a mesh: stream: 32 (over z, y, core), span: 4 (over x).
Axes of the slice: x: 4, y: 4, z: 4, core: 2. Of those that a mesh axis runs over, the one named last changes fastest.
Arguments:
- populations: float32 [19, 1024, 8192], P(None, 'stream', 'span'), as said below
- camera: int32 [32], P('stream'), may hold values from 0 to 1
- active_list: int32 [32, 4, 32], P('stream', 'span'), may hold values from 0 to 32, as said below
- tile_order: int32 [32, 8], P('stream'), may hold values from 0 to 7, each once within a row
Outputs:
- final_populations: float32 [19, 1024, 8192], P(None, 'stream', 'span')
- tile_image: float32 [256, 4, 256], P(('stream', 'span'))
Inputs may be any that keep to these rules, and one draw needn't show every extreme that they name: `active_list`: each row lists the distinct numbers of the active bricks of one device in rising order and then the value 32 in the remaining places; the share of active bricks differs widely between devices, and some device lists all 32 of its bricks. `populations`: populations are positive.
All inputs are finite; a program needn't handle non-finite values.
Results may differ from a plain program's by a relative error of at most 0.0001.
Values sent between devices are 32-bit elements; how exact they have to be, the bound alone decides.
A program may use at most 128 MiB of HBM per device.

v0:
```python
import functools
import math

import jax
import jax.numpy as jnp
from jax import lax
from jax.experimental import pallas as pl
from jax.experimental.pallas import tpu as pltpu
from jax.sharding import PartitionSpec as P

MESH = pl.DeviceIdType.MESH

NZ = 64
LANES = 128
POPS = 19
PLANES = 32
COLUMNS = 16
TOP = 8
ROWS = 48
BLOCKS = PLANES // 8

VELOCITIES = (
    (0, 0, 0),
    (1, 0, 0),
    (-1, 0, 0),
    (0, 1, 0),
    (0, -1, 0),
    (0, 0, 1),
    (0, 0, -1),
    (1, 1, 0),
    (-1, -1, 0),
    (1, -1, 0),
    (-1, 1, 0),
    (1, 0, 1),
    (-1, 0, -1),
    (1, 0, -1),
    (-1, 0, 1),
    (0, 1, 1),
    (0, -1, -1),
    (0, 1, -1),
    (0, -1, 1),
)
OPPOSITE = (0, 2, 1, 4, 3, 6, 5, 8, 7, 10, 9, 12, 11, 14, 13, 16, 15, 18, 17)
TAU_ZERO = 0.55
SMAGORINSKY = 0.17
VORTEX_SCALE = 0.003
SPEED_SCALE = 0.08
OPACITY_GAIN = 0.03

ORDER = (1, 11, 13, 9, 7, 3, 15, 17, 0, 5, 6, 4, 16, 18, 10, 2, 12, 14, 8)
SLOT = tuple(ORDER.index(index) for index in range(POPS))
X_UP, NOT_UP = (0, 5), (5, 14)
X_DOWN, NOT_DOWN = (14, 5), (0, 14)
Y_PACKS = (((7, 3), (15, 17), (10, None)), ((8, 4), (16, 18), (9, None)))

PLACES = COLUMNS + 2
POST_MESSAGES = 8
SPEED_BASE = 3 * POST_MESSAGES
LATE_BASE = SPEED_BASE + 2
TILE_BASE = LATE_BASE + 12
MESSAGES = TILE_BASE + 3


def reciprocal(value):
    return pl.reciprocal(value, approx=True)


def moments(f):
    pair = {index: f[index] + f[index + 1] for index in range(1, POPS, 2)}
    gap = {index: f[index] - f[index + 1] for index in range(1, POPS, 2)}
    flow = (
        (gap[1] + gap[7]) + (gap[9] + gap[11]) + gap[13],
        (gap[3] + gap[7]) + (gap[15] - gap[9]) + gap[17],
        (gap[5] + gap[11]) + (gap[15] - gap[13]) - gap[17],
    )
    around_xy = pair[7] + pair[9]
    around_xz = pair[11] + pair[13]
    around_yz = pair[15] + pair[17]
    along_x = pair[1] + (around_xy + around_xz)
    density = (f[0] + pair[3]) + (pair[5] + around_yz) + along_x
    return pair, flow, (around_xy, around_xz, around_yz), along_x, density


def collide(f):
    pair, flow, around, along_x, density = moments(f)
    along_y = pair[3] + (around[0] + around[2])
    along_z = pair[5] + (around[1] + around[2])
    inverse = reciprocal(density)
    triple = 3.0 * inverse
    ninth = 9.0 * inverse
    vx, vy, vz = [part * triple for part in flow]
    vxx, vyy, vzz = vx * vx, vy * vy, vz * vz
    vxy, vxz, vyz = vx * vy, vx * vz, vy * vz
    qxx = ninth * along_x - (3.0 + vxx)
    qyy = ninth * along_y - (3.0 + vyy)
    qzz = ninth * along_z - (3.0 + vzz)
    qxy = ninth * (pair[7] - pair[9]) - vxy
    qxz = ninth * (pair[11] - pair[13]) - vxz
    qyz = ninth * (pair[15] - pair[17]) - vyz
    cross = qxy * qxy + qxz * qxz + qyz * qyz
    square = (qxx * qxx + qyy * qyy) + (qzz * qzz + (cross + cross))
    magnitude = square * lax.rsqrt(jnp.maximum(square, 1e-30))
    inner = TAU_ZERO * TAU_ZERO + (18.0 * math.sqrt(2.0) * SMAGORINSKY * SMAGORINSKY / 9.0) * magnitude
    rate = 2.0 * reciprocal(TAU_ZERO + inner * lax.rsqrt(inner))
    keep = 1.0 - rate
    weight = (rate * density) * (1.0 / 36.0)
    bx, by, bz = weight * vx, weight * vy, weight * vz
    half = 0.5 * weight
    ax, ay, az = half * vxx, half * vyy, half * vzz
    base = weight - (ax + ay + az) * (1.0 / 3.0)
    ex, ey, ez = base + ax, base + ay, base + az
    out = [None] * POPS
    out[0] = keep * f[0] + 12.0 * base
    for index, even, odd in ((1, ex, bx), (3, ey, by), (5, ez, bz)):
        out[index] = keep * f[index] + 2.0 * (even + odd)
        out[index + 1] = keep * f[index + 1] + 2.0 * (even - odd)
    for index, first, second, middle, mixed in (
        (7, bx, by, ex + ay, weight * vxy),
        (11, bx, bz, ex + az, weight * vxz),
        (15, by, bz, ey + az, weight * vyz),
    ):
        same, other = middle + mixed, middle - mixed
        plus, minus = first + second, first - second
        out[index] = keep * f[index] + (same + plus)
        out[index + 1] = keep * f[index + 1] + (same - plus)
        out[index + 2] = keep * f[index + 2] + (other + minus)
        out[index + 3] = keep * f[index + 3] + (other - minus)
    return out


def kernel(
    spans,
    streams,
    populations,
    camera_in,
    active_in,
    order_in,
    final,
    tile_image,
    camera,
    active_list,
    tile_order,
    field,
    post0,
    post1,
    post2,
    speed,
    strips,
    deep,
    second,
    rims,
    arrived,
    speed_rims,
    foot,
    outgoing,
    incoming,
    send_sem,
    recv_sem,
    load_sem,
    own_sem,
    small_sem,
):
    stream = lax.axis_index("stream")
    span = lax.axis_index("span")
    stream_up = lax.rem(stream + 1, streams)
    stream_down = lax.rem(stream + streams - 1, streams)
    span_up = lax.rem(span + 1, spans)
    span_down = lax.rem(span + spans - 1, spans)
    span_far = lax.rem(span + 2, spans)

    barrier = pltpu.get_barrier_semaphore()
    partners = (
        (stream_up, span),
        (stream_down, span),
        (stream, span_up),
        (stream, span_down),
        (stream_up, span_up),
        (stream_up, span_down),
        (stream_down, span_up),
        (stream_down, span_down),
        (stream, span_far),
    )
    for partner in partners:
        pl.semaphore_signal(barrier, inc=1, device_id=partner, device_id_type=MESH)

    loads = [None] * COLUMNS
    for k in range(COLUMNS // 2):
        for column in (k, COLUMNS - 1 - k):
            loads[column] = pltpu.make_async_copy(
                populations.at[:, :, pl.ds(column * LANES, LANES)], field.at[:, column], load_sem.at[column]
            )
            loads[column].start()
    small = [
        pltpu.make_async_copy(source, target, small_sem.at[number])
        for number, (source, target) in enumerate(
            ((camera_in, camera), (active_in, active_list), (order_in, tile_order))
        )
    ]
    for copy in small:
        copy.start()

    lane = lax.broadcasted_iota(jnp.int32, (8, LANES), 1)
    upper = lane >= NZ
    level = lax.rem(lane, NZ)
    floor = level == 0
    ceiling = level == NZ - 1

    def remote(source, target, number, device):
        return pltpu.make_async_remote_copy(
            src_ref=source,
            dst_ref=target,
            send_sem=send_sem.at[number],
            recv_sem=recv_sem.at[number],
            device_id=device,
            device_id_type=MESH,
        )

    before_row, after_row = TOP - 1, TOP + PLANES
    before_place, after_place = 0, PLACES - 1

    def x_copies(buffer, up_strip, down_strip, up, down, depth, number):
        places = pl.ds(1, COLUMNS)
        return [
            remote(up_strip, buffer.at[pl.ds(*up), places, before_row - depth], number, (stream_up, span)),
            remote(down_strip, buffer.at[pl.ds(*down), places, after_row + depth], number + 1, (stream_down, span)),
        ]

    def y_copies(up_source, up_target, down_source, down_target, number):
        return [
            remote(up_source, up_target, number, (stream, span_up)),
            remote(down_source, down_target, number + 1, (stream, span_down)),
        ]

    corner_paths = (
        (7, 0, COLUMNS - 1, before_place, before_row, (stream_up, span_up)),
        (9, 0, 0, after_place, before_row, (stream_up, span_down)),
        (10, 1, COLUMNS - 1, before_place, after_row, (stream_down, span_up)),
        (8, 1, 0, after_place, after_row, (stream_down, span_down)),
    )

    def corner_copies(buffer, strip, number, first, count=1, depth=0):
        copies = []
        for index, side, column, place, row, device in corner_paths:
            slot = SLOT[index] if count == 1 else SLOT[3 if column else 4]
            outwards = -depth if row == before_row else depth
            copies.append(
                remote(
                    strip[side].at[pl.ds(slot - first[side], count), pl.ds(column, 1)],
                    buffer.at[pl.ds(slot, count), place, pl.ds(row + outwards, 1)],
                    number + len(copies),
                    device,
                )
            )
        return copies

    def joined(along_y, before, here, after):
        if along_y == 1:
            return jnp.where(upper, before(), here())
        if along_y == -1:
            return jnp.where(upper, here(), after())
        return here()

    def block_reader(buffer, place, block):
        def read(slot, along_y, plane):
            rows = pl.ds(TOP + 8 * block + plane, 8)
            return joined(
                along_y,
                lambda: buffer[slot, place - 1, rows],
                lambda: buffer[slot, place, rows],
                lambda: buffer[slot, place + 1, rows],
            )

        return read

    def strip_reader(buffer, plane, half):
        flat = buffer.reshape(buffer.shape[0], PLACES * ROWS, LANES)
        first = (8 * half + 1) * ROWS + TOP + plane

        def read(slot, along_y, along):
            def at(step):
                return lambda: flat[slot, pl.ds(first + step * ROWS + along, 8, stride=ROWS)]

            return joined(along_y, at(-1), at(0), at(1))

        return read

    def rim_reader(buffer, block):
        def read(slot, along_y, plane):
            rows = pl.ds(TOP + 8 * block + plane, 8)
            high, low = {0: (COLUMNS, 1), 1: (0, COLUMNS), -1: (1, PLACES - 1)}[along_y]
            return jnp.where(upper, buffer[slot, high, rows], buffer[slot, low, rows])

        return read

    def streamed(read):
        values = []
        for index in range(POPS):
            along_x, along_y, along_z = VELOCITIES[index]
            value = read(SLOT[index], along_y, -along_x)
            shift = ((NZ if along_y else 0) + along_z) % LANES
            if shift:
                value = pltpu.roll(value, shift, 1)
            if along_z:
                value = jnp.where(
                    floor if along_z > 0 else ceiling, read(SLOT[OPPOSITE[index]], 0, 0), value
                )
            values.append(value)
        return values

    def sweep(work, first, last, step, blocks):
        def body(k, carry):
            for part in range(step):
                work(first + step * k + part, blocks)
            return carry

        lax.fori_loop(0, (last - first) // step, body, 0)

    everything = tuple(range(BLOCKS))

    def inner(work):
        sweep(work, 1, COLUMNS - 1, 7, (1, 2))

    def outer(work):
        for column in (0, COLUMNS - 1):
            work(column, (1, 2))
        sweep(work, 0, COLUMNS, 8, (0, 3))

    sent = []

    def send(copies):
        for copy in copies:
            copy.start()
        sent.extend(copies)

    buffers = (post0, post1, post2)
    edge_strips = [(strips.at[phase, 0], strips.at[phase, 1]) for phase in range(2)]
    edge_strips.append((deep.at[0, pl.ds(*X_UP)], deep.at[1, pl.ds(*X_DOWN)]))
    x_sides, corners = [], []
    for phase, buffer in enumerate(buffers):
        number = phase * POST_MESSAGES
        x_sides.append(x_copies(buffer, *edge_strips[phase], X_UP, X_DOWN, 0, number))
        if phase < 2:
            corners.append(
                corner_copies(buffer, edge_strips[phase], number + 2, (X_UP[0], X_DOWN[0]))
            )
        else:
            corners.append(corner_copies(buffer, (deep.at[0], deep.at[1]), number + 2, (0, 0)))
    late = x_copies(
        post2, deep.at[0, pl.ds(*NOT_UP)], deep.at[1, pl.ds(*NOT_DOWN)], NOT_UP, NOT_DOWN, 0, LATE_BASE
    )
    late += x_copies(post2, second.at[0], second.at[1], X_UP, X_DOWN, 1, LATE_BASE + 2)
    late += corner_copies(post2, (deep.at[0], deep.at[1]), LATE_BASE + 4, (0, 0), count=3)
    late += corner_copies(
        post2, (second.at[0], second.at[1]), LATE_BASE + 8, (X_UP[0], X_DOWN[0]), depth=1
    )
    y_sides = [
        y_copies(
            rims.at[phase, 0],
            arrived.at[phase, 0],
            rims.at[phase, 1],
            arrived.at[phase, 1],
            phase * POST_MESSAGES + 6,
        )
        for phase in range(3)
    ]

    def post_strips(values_of, planes, store):
        for side in range(2):
            for half in range(2):
                out = collide(values_of(planes[side], half))
                store(side, pl.ds(8 * half, 8), out)

    def store_edges(phase):
        def store(side, rows, out):
            first, count = (X_UP, X_DOWN)[side]
            for place in range(count):
                strips[phase, side, place, rows] = out[ORDER[first + place]]

        return store

    def store_deep(side, rows, out):
        for index in range(POPS):
            deep[side, SLOT[index], rows] = out[index]

    def store_second(side, rows, out):
        first, count = (X_UP, X_DOWN)[side]
        for place in range(count):
            second[side, place, rows] = out[ORDER[first + place]]

    edge_planes, second_planes = (PLANES - 1, 0), (PLANES - 2, 1)

    def post_rims(phase, values_of):
        for block in range(BLOCKS):
            out = collide(values_of(block))
            rows = pl.ds(8 * block, 8)
            for side in range(2):
                for pack, (first, second) in enumerate(Y_PACKS[side]):
                    value = out[first]
                    if second is not None:
                        other = pltpu.roll(out[second], NZ, 1)
                        value = jnp.where(upper, other, value) if side else jnp.where(upper, value, other)
                    rims[phase, side, pack, rows] = value

    def await_rims(phase):
        for copy in x_sides[phase] + corners[phase] + y_sides[phase]:
            copy.wait_recv()
        for side, place in enumerate((before_place, after_place)):
            for pack, (first, second) in enumerate(Y_PACKS[side]):
                for block in range(BLOCKS):
                    value = arrived[phase, side, pack, pl.ds(8 * block, 8)]
                    rows = pl.ds(TOP + 8 * block, 8)
                    buffers[phase][SLOT[first], place, rows] = value
                    if second is not None:
                        buffers[phase][SLOT[second], place, rows] = pltpu.roll(value, NZ, 1)

    def post_column(target, column, blocks, values_of):
        for block in blocks:
            out = collide(values_of(block))
            for index in range(POPS):
                target[SLOT[index], column + 1, pl.ds(TOP + 8 * block, 8)] = out[index]

    def first_work(column, blocks):
        post_column(
            post0,
            column,
            blocks,
            lambda block: [field[index, column, pl.ds(8 * block, 8)] for index in range(POPS)],
        )

    for column in (0, COLUMNS - 1):
        loads[column].wait()
    post_rims(
        0,
        lambda block: [
            jnp.where(upper, field[index, COLUMNS - 1, pl.ds(8 * block, 8)], field[index, 0, pl.ds(8 * block, 8)])
            for index in range(POPS)
        ],
    )
    for column in range(1, COLUMNS - 1):
        loads[column].wait()
    flat_field = field.reshape(POPS, COLUMNS * PLANES, LANES)
    post_strips(
        lambda plane, half: [
            flat_field[index, pl.ds(8 * half * PLANES + plane, 8, stride=PLANES)] for index in range(POPS)
        ],
        edge_planes,
        store_edges(0),
    )
    pl.semaphore_wait(barrier, len(partners))
    send(x_sides[0] + corners[0] + y_sides[0])
    sweep(first_work, 0, COLUMNS, 4, everything)

    for phase in (1, 2):
        source, target = buffers[phase - 1], buffers[phase]

        def step_work(column, blocks):
            post_column(target, column, blocks, lambda block: streamed(block_reader(source, column + 1, block)))

        def strip_values(plane, half):
            return streamed(strip_reader(source, plane, half))

        inner(step_work)
        await_rims(phase - 1)
        post_strips(strip_values, edge_planes, store_edges(phase) if phase == 1 else store_deep)
        send(x_sides[phase] + corners[phase])
        post_rims(phase, lambda block: streamed(rim_reader(source, block)))
        send(y_sides[phase])
        if phase == 2:
            post_strips(strip_values, second_planes, store_second)
            send(late)
        outer(step_work)

    def velocity(values):
        _, flow, _, _, density = moments(values)
        inverse = reciprocal(density)
        return [part * inverse for part in flow]

    def last_work(column, blocks):
        lanes = pl.ds(pl.multiple_of(column * LANES, LANES), LANES)
        for block in blocks:
            values = streamed(block_reader(post2, column + 1, block))
            for index in range(POPS):
                final[index, pl.ds(8 * block, 8), lanes] = values[index]
            for dimension, part in enumerate(velocity(values)):
                speed[dimension, column + 1, pl.ds(TOP + 8 * block, 8)] = part

    inner(last_work)
    await_rims(2)
    for block in range(BLOCKS):
        for dimension, part in enumerate(velocity(streamed(rim_reader(post2, block)))):
            speed_rims[dimension, pl.ds(8 * block, 8)] = part
    rows = pl.ds(TOP, PLANES)
    speed_y = y_copies(
        speed_rims, speed.at[:, before_place, rows], speed_rims, speed.at[:, after_place, rows], SPEED_BASE
    )
    send(speed_y)
    outer(last_work)

    for copy in small:
        copy.wait()

    bits = jnp.int32(0)
    for entry in range(32):
        number = active_list[entry]
        bits = bits | jnp.where(number < 32, jnp.left_shift(jnp.int32(1), jnp.minimum(number, 31)), 0)
    falling = jnp.full((8, LANES), camera[0], jnp.int32) == 1
    leading = falling == upper
    bits = jnp.full((8, LANES), bits, jnp.int32)
    corner = 4 * (lax.broadcasted_iota(jnp.int32, (8, LANES), 0) // 4)

    def ray(k, side, block, sums):
        column = k if side == 0 else COLUMNS - 1 - k
        read = block_reader(speed, column + 1, block)
        centre = [read(dimension, 0, 0) for dimension in range(3)]
        slope_x, slope_y, slope_z = [], [], []
        for dimension in range(3):
            here = centre[dimension]
            slope_x.append(read(dimension, 0, 1) - read(dimension, 0, -1))
            slope_y.append(pltpu.roll(read(dimension, -1, 0) - read(dimension, 1, 0), NZ, 1))
            above = jnp.where(ceiling, -here, pltpu.roll(here, LANES - 1, 1))
            below = jnp.where(floor, -here, pltpu.roll(here, 1, 1))
            slope_z.append(above - below)
        cross = slope_x[1] * slope_y[0] + slope_x[2] * slope_z[0] + slope_y[2] * slope_z[1]
        total = slope_x[0] * slope_x[0] + slope_y[1] * slope_y[1] + slope_z[2] * slope_z[2] + (cross + cross)
        vortex = total * (-0.125 / VORTEX_SCALE)
        small = jnp.exp(-jnp.abs(vortex))
        one = 1.0 + small
        share = reciprocal(one)
        colours = [jnp.where(vortex >= 0.0, share, small * share)]
        for dimension in (0, 2):
            colours.append(reciprocal(1.0 + jnp.exp(centre[dimension] * (-1.0 / SPEED_SCALE))))
        passing = jnp.exp(-OPACITY_GAIN * (jnp.maximum(vortex, 0.0) + jnp.log(one)))
        brick = corner + (8 * block + column // 4)
        passing = jnp.where((jnp.right_shift(bits, brick) & 1) == 1, passing, 1.0)
        opacity = 1.0 - passing
        other = pltpu.roll(passing, NZ, 1)
        both = passing * other
        weight = opacity * jnp.where(leading, 1.0, other)
        from_back = falling if side == 1 else jnp.logical_not(falling)
        through = sums[3]
        weight = weight * jnp.where(from_back, 1.0, through)
        fade = jnp.where(from_back, both, 1.0)
        return tuple(sums[n] * fade + colours[n] * weight for n in range(3)) + (through * both,)

    start = tuple(jnp.zeros((8, LANES), jnp.float32) for _ in range(3)) + (jnp.ones((8, LANES), jnp.float32),)
    sums = {(side, block): start for side in range(2) for block in range(BLOCKS)}

    def walk(blocks):
        for k in range(COLUMNS // 2 - 1, 0, -1):
            for side in range(2):
                for block in blocks:
                    sums[side, block] = ray(k, side, block, sums[side, block])

    walk((1, 2))
    for copy in late:
        copy.wait_recv()
    flat_speed = speed.reshape(3, PLACES * ROWS, LANES)
    for plane in (-1, PLANES):
        for half in range(2):
            for dimension, part in enumerate(velocity(streamed(strip_reader(post2, plane, half)))):
                first = (8 * half + 1) * ROWS + TOP + plane
                flat_speed[dimension, pl.ds(first, 8, stride=ROWS)] = part
    walk((0, 3))
    for copy in speed_y:
        copy.wait_recv()
    for key in sums:
        sums[key] = ray(0, key[0], key[1], sums[key])

    for block in range(BLOCKS):
        low, high = sums[0, block], sums[1, block]
        front = [jnp.where(falling, b, a) for a, b in zip(low, high)]
        back = [jnp.where(falling, a, b) for a, b in zip(low, high)]
        for number in range(4):
            if number < 3:
                half = front[number] + front[3] * back[number]
                value = half + pltpu.roll(half, NZ, 1)
            else:
                value = front[3] * back[3]
            for part in range(2):
                foot[2 * block + part, pl.ds(4 * number, 4)] = value[4 * part : 4 * part + 4]

    for number in range(8):
        outgoing[number] = foot[tile_order[number]]
    tiles = []
    for hop, target in enumerate((span_up, span_down, span_far)):
        tiles.append(
            remote(
                outgoing.at[pl.ds(2 * target, 2)], incoming.at[span], TILE_BASE + hop, (stream, target)
            )
        )
    earlier = list(sent)
    send(tiles)
    own = pltpu.make_async_copy(outgoing.at[pl.ds(2 * span, 2)], incoming.at[span], own_sem)
    own.start()
    own.wait()
    for copy in earlier:
        copy.wait_send()
    for copy in tiles:
        copy.wait_recv()
    wide = jnp.broadcast_to(camera[0], (16, LANES)) == 1
    upper_row = lax.broadcasted_iota(jnp.int32, (1, LANES), 1) >= NZ
    for tile in range(2):
        sheets = [incoming[source, tile] for source in range(spans)]
        colour = sheets[0][:12]
        through = sheets[0][12:]
        for source in range(1, spans):
            sheet = sheets[source]
            fade = jnp.concatenate([sheet[12:]] * 3, axis=0)
            veil = jnp.concatenate([through] * 3, axis=0)
            colour = jnp.where(wide[:12], colour * fade + sheet[:12], colour + veil * sheet[:12])
            through = through * sheet[12:]
        for number in range(4):
            quad = colour[4 * number : 4 * number + 4] if number < 3 else through
            for part in range(2):
                tile_image[tile, pl.ds(number, 1), pl.ds(part * LANES, LANES)] = jnp.where(
                    upper_row, quad[2 * part + 1 : 2 * part + 2], quad[2 * part : 2 * part + 1]
                )

    for copy in tiles:
        copy.wait_send()


def store_kernel(final, tile_image, final_out, image_out, sems):
    copies = [
        pltpu.make_async_copy(final.at[index], final_out.at[index], sems.at[index]) for index in range(POPS)
    ]
    copies.append(pltpu.make_async_copy(tile_image, image_out, sems.at[POPS]))
    for copy in copies:
        copy.start()
    for copy in copies:
        copy.wait()


def on_device(populations, camera, active_list, tile_order):
    spans = lax.axis_size("span")
    streams = lax.axis_size("stream")
    vmem = functools.partial(pl.BlockSpec, memory_space=pltpu.VMEM)
    pinned = functools.partial(pltpu.with_memory_space_constraint, memory_space=pltpu.HBM)
    anywhere = functools.partial(pl.BlockSpec, memory_space=pl.ANY)
    post = pltpu.VMEM((POPS, PLACES, ROWS, LANES), jnp.float32)
    final, tile_image = pl.pallas_call(
        functools.partial(kernel, spans, streams),
        out_shape=(
            jax.ShapeDtypeStruct(populations.shape, jnp.float32),
            jax.ShapeDtypeStruct((2, 4, 256), jnp.float32),
        ),
        in_specs=[anywhere()] * 4,
        out_specs=(vmem(), vmem()),
        scratch_shapes=[
            pltpu.SMEM(camera.shape, jnp.int32),
            pltpu.SMEM((active_list.size,), jnp.int32),
            pltpu.SMEM((tile_order.size,), jnp.int32),
            pltpu.VMEM((POPS, COLUMNS, PLANES, LANES), jnp.float32),
            post,
            post,
            post,
            pltpu.VMEM((3, PLACES, ROWS, LANES), jnp.float32),
            pltpu.VMEM((2, 2, 5, COLUMNS, LANES), jnp.float32),
            pltpu.VMEM((2, POPS, COLUMNS, LANES), jnp.float32),
            pltpu.VMEM((2, 5, COLUMNS, LANES), jnp.float32),
            pltpu.VMEM((3, 2, 3, PLANES, LANES), jnp.float32),
            pltpu.VMEM((3, 2, 3, PLANES, LANES), jnp.float32),
            pltpu.VMEM((3, PLANES, LANES), jnp.float32),
            pltpu.VMEM((8, 16, LANES), jnp.float32),
            pltpu.VMEM((8, 16, LANES), jnp.float32),
            pltpu.VMEM((spans, 2, 16, LANES), jnp.float32),
            pltpu.SemaphoreType.DMA((MESSAGES,)),
            pltpu.SemaphoreType.DMA((MESSAGES,)),
            pltpu.SemaphoreType.DMA((COLUMNS,)),
            pltpu.SemaphoreType.DMA,
            pltpu.SemaphoreType.DMA((3,)),
        ],
        compiler_params=pltpu.CompilerParams(
            collective_id=0, has_side_effects=True, vmem_limit_bytes=48 * 1024 * 1024
        ),
    )(populations, camera, pinned(active_list.reshape(-1)), pinned(tile_order.reshape(-1)))
    return pl.pallas_call(
        store_kernel,
        out_shape=(
            jax.ShapeDtypeStruct(final.shape, jnp.float32),
            jax.ShapeDtypeStruct(tile_image.shape, jnp.float32),
        ),
        in_specs=[anywhere()] * 2,
        out_specs=(anywhere(), anywhere()),
        scratch_shapes=[pltpu.SemaphoreType.DMA((POPS + 1,))],
        compiler_params=pltpu.CompilerParams(vmem_limit_bytes=1024 * 1024),
    )(final, tile_image)


def solution(mesh):
    placed = (P(None, "stream", "span"), P("stream"), P("stream", "span", None), P("stream", None))
    return jax.shard_map(
        on_device,
        mesh=mesh,
        in_specs=placed,
        out_specs=(P(None, "stream", "span"), P(("stream", "span"), None, None)),
        check_vma=False,
    )
```

profile of v0, /device:TPU:0, one launch (start us, length us, event | category | flops | bytes accessed | tf_op | source)
XLA Modules:
  0.0 35.2 jit_solution(1211884800303211892)
XLA Ops:
  1.3 31.5 %shard_map.59 = (f32[19,32,2048]{2,1,0:T(8,128)S(1)}, f32[2,4,256]{2,1,0:T(4,128)S(1)}) custom-call(f32[19,32,2048]{2,1,0:T(8,128)} %populations.1, s32[1]{0:T(128)S(6)} %copy.6.camera_in, s32[32]{0:T(128)} %bitcast.2, s32[8]{0:T(128)} %bitcast.3), custom_call_target="tpu_custom_call" | custom-call | tf_op jit(solution)/shard_map/pallas_call | solution.py:641
  32.8 2.4 %shard_map.60 = (f32[19,32,2048]{2,1,0:T(8,128)}, f32[2,4,256]{2,1,0:T(4,128)}) custom-call(f32[19,32,2048]{2,1,0:T(8,128)S(1)} %get-tuple-element.4.final, f32[2,4,256]{2,1,0:T(4,128)S(1)} %get-tuple-element.5.tile_image), custom_call_target="tpu_custom_call" | custom-call | tf_op jit(solution)/shard_map/pallas_call | solution.py:677
where the time goes:
time: 35.4 us; the launch traced here: 35.2 us
  Pallas kernels  34 us (96%)
  between operations  1.28 us (4%)
    pallas_call x1, Pallas kernels, on_device(): pl.pallas_call(functools.partial(kernel, spans, streams), out_shape=(jax....  31.5 us
    pallas_call x1, Pallas kernels, on_device(): pl.pallas_call(store_kernel, out_shape=(jax.ShapeDtypeStruct(final.shape,...  2.42 us

commit v1 on v0

--- a/solution.py
+++ b/solution.py
@@ -47,11 +47,14 @@
 SPEED_SCALE = 0.08
 OPACITY_GAIN = 0.03
 
-ORDER = (1, 11, 13, 9, 7, 3, 15, 17, 0, 5, 6, 4, 16, 18, 10, 2, 12, 14, 8)
+ORDER = (1, 9, 7, 11, 13, 3, 15, 17, 0, 5, 6, 4, 16, 18, 12, 14, 10, 2, 8)
 SLOT = tuple(ORDER.index(index) for index in range(POPS))
-X_UP, NOT_UP = (0, 5), (5, 14)
-X_DOWN, NOT_DOWN = (14, 5), (0, 14)
-Y_PACKS = (((7, 3), (15, 17), (10, None)), ((8, 4), (16, 18), (9, None)))
+X_UP, LATE_UP = (0, 5), (5, 11)
+X_DOWN, LATE_DOWN = (14, 5), (3, 11)
+Y_PACKS = (((7, 3), (15, 17)), ((8, 4), (16, 18)))
+Y_ALONE = (10, 9)
+RIM_ROWS = 2 * PLANES + PLANES // 2
+SPEED_ROWS = PLANES + PLANES // 2
 
 PLACES = COLUMNS + 2
 POST_MESSAGES = 8
@@ -151,6 +154,8 @@
     rims,
     arrived,
     speed_rims,
+    speed_arrived,
+    shaded,
     foot,
     outgoing,
     incoming,
@@ -272,9 +277,9 @@
 
         return read
 
-    def strip_reader(buffer, plane, half):
+    def strip_reader(buffer, plane, column):
         flat = buffer.reshape(buffer.shape[0], PLACES * ROWS, LANES)
-        first = (8 * half + 1) * ROWS + TOP + plane
+        first = (column + 1) * ROWS + TOP + plane
 
         def read(slot, along_y, along):
             def at(step):
@@ -307,18 +312,18 @@
             values.append(value)
         return values
 
-    def sweep(work, first, last, step, blocks):
+    def sweep(work, first, last, step, blocks, start=0, stop=None):
         def body(k, carry):
             for part in range(step):
                 work(first + step * k + part, blocks)
             return carry
 
-        lax.fori_loop(0, (last - first) // step, body, 0)
+        lax.fori_loop(start, (last - first) // step if stop is None else stop, body, 0)
 
     everything = tuple(range(BLOCKS))
 
-    def inner(work):
-        sweep(work, 1, COLUMNS - 1, 7, (1, 2))
+    def inner(work, start=0, stop=None):
+        sweep(work, 1, COLUMNS - 1, 7, (1, 2), start, stop)
 
     def outer(work):
         for column in (0, COLUMNS - 1):
@@ -346,7 +351,7 @@
         else:
             corners.append(corner_copies(buffer, (deep.at[0], deep.at[1]), number + 2, (0, 0)))
     late = x_copies(
-        post2, deep.at[0, pl.ds(*NOT_UP)], deep.at[1, pl.ds(*NOT_DOWN)], NOT_UP, NOT_DOWN, 0, LATE_BASE
+        post2, deep.at[0, pl.ds(*LATE_UP)], deep.at[1, pl.ds(*LATE_DOWN)], LATE_UP, LATE_DOWN, 0, LATE_BASE
     )
     late += x_copies(post2, second.at[0], second.at[1], X_UP, X_DOWN, 1, LATE_BASE + 2)
     late += corner_copies(post2, (deep.at[0], deep.at[1]), LATE_BASE + 4, (0, 0), count=3)
@@ -367,7 +372,7 @@
     def post_strips(values_of, planes, store):
         for side in range(2):
             for half in range(2):
-                out = collide(values_of(planes[side], half))
+                out = collide(values_of(planes[side], 8 * half))
                 store(side, pl.ds(8 * half, 8), out)
 
     def store_edges(phase):
@@ -389,29 +394,40 @@
 
     edge_planes, second_planes = (PLANES - 1, 0), (PLANES - 2, 1)
 
+    def packed(side, own, other):
+        turned = pltpu.roll(other, NZ, 1)
+        return jnp.where(upper, turned, own) if side else jnp.where(upper, own, turned)
+
     def post_rims(phase, values_of):
+        alone = []
         for block in range(BLOCKS):
             out = collide(values_of(block))
-            rows = pl.ds(8 * block, 8)
             for side in range(2):
                 for pack, (first, second) in enumerate(Y_PACKS[side]):
-                    value = out[first]
-                    if second is not None:
-                        other = pltpu.roll(out[second], NZ, 1)
-                        value = jnp.where(upper, other, value) if side else jnp.where(upper, value, other)
-                    rims[phase, side, pack, rows] = value
+                    rims[phase, side, pl.ds(pack * PLANES + 8 * block, 8)] = packed(side, out[first], out[second])
+            alone.append([out[index] for index in Y_ALONE])
+        for block in range(BLOCKS // 2):
+            for side in range(2):
+                rims[phase, side, pl.ds(2 * PLANES + 8 * block, 8)] = packed(
+                    side, alone[block][side], alone[block + BLOCKS // 2][side]
+                )
 
     def await_rims(phase):
         for copy in x_sides[phase] + corners[phase] + y_sides[phase]:
             copy.wait_recv()
+        buffer = buffers[phase]
         for side, place in enumerate((before_place, after_place)):
-            for pack, (first, second) in enumerate(Y_PACKS[side]):
-                for block in range(BLOCKS):
-                    value = arrived[phase, side, pack, pl.ds(8 * block, 8)]
-                    rows = pl.ds(TOP + 8 * block, 8)
-                    buffers[phase][SLOT[first], place, rows] = value
-                    if second is not None:
-                        buffers[phase][SLOT[second], place, rows] = pltpu.roll(value, NZ, 1)
+            for block in range(BLOCKS):
+                rows = pl.ds(TOP + 8 * block, 8)
+                for pack, (first, second) in enumerate(Y_PACKS[side]):
+                    value = arrived[phase, side, pl.ds(pack * PLANES + 8 * block, 8)]
+                    buffer[SLOT[first], place, rows] = value
+                    buffer[SLOT[second], place, rows] = pltpu.roll(value, NZ, 1)
+            for block in range(BLOCKS // 2):
+                value = arrived[phase, side, pl.ds(2 * PLANES + 8 * block, 8)]
+                slot = SLOT[Y_ALONE[side]]
+                buffer[slot, place, pl.ds(TOP + 8 * block, 8)] = value
+                buffer[slot, place, pl.ds(TOP + PLANES // 2 + 8 * block, 8)] = pltpu.roll(value, NZ, 1)
 
     def post_column(target, column, blocks, values_of):
         for block in blocks:
@@ -440,15 +456,17 @@
         loads[column].wait()
     flat_field = field.reshape(POPS, COLUMNS * PLANES, LANES)
     post_strips(
-        lambda plane, half: [
-            flat_field[index, pl.ds(8 * half * PLANES + plane, 8, stride=PLANES)] for index in range(POPS)
+        lambda plane, column: [
+            flat_field[index, pl.ds(column * PLANES + plane, 8, stride=PLANES)] for index in range(POPS)
         ],
         edge_planes,
         store_edges(0),
     )
+    seam = (stream == 0).astype(jnp.int32)
+    sweep(first_work, 0, COLUMNS, 4, everything, 0, 4 * seam)
     pl.semaphore_wait(barrier, len(partners))
     send(x_sides[0] + corners[0] + y_sides[0])
-    sweep(first_work, 0, COLUMNS, 4, everything)
+    sweep(first_work, 0, COLUMNS, 4, everything, 4 * seam)
 
     for phase in (1, 2):
         source, target = buffers[phase - 1], buffers[phase]
@@ -456,18 +474,18 @@
         def step_work(column, blocks):
             post_column(target, column, blocks, lambda block: streamed(block_reader(source, column + 1, block)))
 
-        def strip_values(plane, half):
-            return streamed(strip_reader(source, plane, half))
+        def strip_values(plane, column):
+            return streamed(strip_reader(source, plane, column))
 
         inner(step_work)
         await_rims(phase - 1)
         post_strips(strip_values, edge_planes, store_edges(phase) if phase == 1 else store_deep)
         send(x_sides[phase] + corners[phase])
-        post_rims(phase, lambda block: streamed(rim_reader(source, block)))
-        send(y_sides[phase])
         if phase == 2:
             post_strips(strip_values, second_planes, store_second)
             send(late)
+        post_rims(phase, lambda block: streamed(rim_reader(source, block)))
+        send(y_sides[phase])
         outer(step_work)
 
     def velocity(values):
@@ -486,12 +504,16 @@
 
     inner(last_work)
     await_rims(2)
-    for block in range(BLOCKS):
-        for dimension, part in enumerate(velocity(streamed(rim_reader(post2, block)))):
-            speed_rims[dimension, pl.ds(8 * block, 8)] = part
-    rows = pl.ds(TOP, PLANES)
+    parts = [velocity(streamed(rim_reader(post2, block))) for block in range(BLOCKS)]
+    for side in range(2):
+        for block in range(BLOCKS):
+            speed_rims[side, pl.ds(8 * block, 8)] = packed(side, parts[block][0], parts[block][1])
+        for block in range(BLOCKS // 2):
+            speed_rims[side, pl.ds(PLANES + 8 * block, 8)] = packed(
+                side, parts[block][2], parts[block + BLOCKS // 2][2]
+            )
     speed_y = y_copies(
-        speed_rims, speed.at[:, before_place, rows], speed_rims, speed.at[:, after_place, rows], SPEED_BASE
+        speed_rims.at[0], speed_arrived.at[0], speed_rims.at[1], speed_arrived.at[1], SPEED_BASE
     )
     send(speed_y)
     outer(last_work)
@@ -508,9 +530,7 @@
     bits = jnp.full((8, LANES), bits, jnp.int32)
     corner = 4 * (lax.broadcasted_iota(jnp.int32, (8, LANES), 0) // 4)
 
-    def ray(k, side, block, sums):
-        column = k if side == 0 else COLUMNS - 1 - k
-        read = block_reader(speed, column + 1, block)
+    def shade_with(read, brick, store):
         centre = [read(dimension, 0, 0) for dimension in range(3)]
         slope_x, slope_y, slope_z = [], [], []
         for dimension in range(3):
@@ -530,41 +550,79 @@
         for dimension in (0, 2):
             colours.append(reciprocal(1.0 + jnp.exp(centre[dimension] * (-1.0 / SPEED_SCALE))))
         passing = jnp.exp(-OPACITY_GAIN * (jnp.maximum(vortex, 0.0) + jnp.log(one)))
-        brick = corner + (8 * block + column // 4)
         passing = jnp.where((jnp.right_shift(bits, brick) & 1) == 1, passing, 1.0)
-        opacity = 1.0 - passing
         other = pltpu.roll(passing, NZ, 1)
-        both = passing * other
-        weight = opacity * jnp.where(leading, 1.0, other)
-        from_back = falling if side == 1 else jnp.logical_not(falling)
-        through = sums[3]
-        weight = weight * jnp.where(from_back, 1.0, through)
-        fade = jnp.where(from_back, both, 1.0)
-        return tuple(sums[n] * fade + colours[n] * weight for n in range(3)) + (through * both,)
-
-    start = tuple(jnp.zeros((8, LANES), jnp.float32) for _ in range(3)) + (jnp.ones((8, LANES), jnp.float32),)
-    sums = {(side, block): start for side in range(2) for block in range(BLOCKS)}
-
-    def walk(blocks):
-        for k in range(COLUMNS // 2 - 1, 0, -1):
-            for side in range(2):
-                for block in blocks:
-                    sums[side, block] = ray(k, side, block, sums[side, block])
-
-    walk((1, 2))
+        weight = (1.0 - passing) * jnp.where(leading, 1.0, other)
+        for number in range(3):
+            store(number, colours[number] * weight)
+        store(3, passing * other)
+
+    def shade(column, blocks):
+        for block in blocks:
+
+            def store(number, value):
+                shaded[number, column, pl.ds(8 * block, 8)] = value
+
+            shade_with(block_reader(speed, column + 1, block), corner + (8 * block + column // 4), store)
+
+    flat_shaded = shaded.reshape(4, COLUMNS * PLANES, LANES)
+
+    def shade_strip(plane, first):
+        def store(number, value):
+            flat_shaded[number, pl.ds(first * PLANES + plane, 8, stride=PLANES)] = value
+
+        brick = (lax.broadcasted_iota(jnp.int32, (8, LANES), 0) + first) // 4
+        shade_with(strip_reader(speed, plane, first), brick + plane // 4 * 4, store)
+
+    for plane in (-1, PLANES):
+        for place in range(1, COLUMNS + 1):
+            speed[:, place, pl.ds(TOP + plane, 1)] = jnp.zeros((3, 1, LANES), jnp.float32)
+    sweep(shade, 1, COLUMNS - 1, 7, (1, 2))
+    sweep(shade, 1, COLUMNS - 1, 7, (0, 3))
     for copy in late:
         copy.wait_recv()
     flat_speed = speed.reshape(3, PLACES * ROWS, LANES)
     for plane in (-1, PLANES):
-        for half in range(2):
-            for dimension, part in enumerate(velocity(streamed(strip_reader(post2, plane, half)))):
-                first = (8 * half + 1) * ROWS + TOP + plane
-                flat_speed[dimension, pl.ds(first, 8, stride=ROWS)] = part
-    walk((0, 3))
+        for first in (0, 8):
+            for dimension, part in enumerate(velocity(streamed(strip_reader(post2, plane, first)))):
+                flat_speed[dimension, pl.ds((first + 1) * ROWS + TOP + plane, 8, stride=ROWS)] = part
+    for plane in (0, PLANES - 1):
+        for first in (1, 7):
+            shade_strip(plane, first)
+
+    def walk(side, block, first, last, state):
+        from_back = falling if side == 1 else jnp.logical_not(falling)
+        colours, through = state[:3], state[3]
+        for k in range(first, last, -1):
+            column = k if side == 0 else COLUMNS - 1 - k
+            pair = [shaded[number, column, pl.ds(8 * block, 8)] for number in range(4)]
+            fade = jnp.where(from_back, pair[3], 1.0)
+            veil = jnp.where(from_back, 1.0, through)
+            colours = [colours[number] * fade + pair[number] * veil for number in range(3)]
+            through = through * pair[3]
+        return colours + [through]
+
+    sums = {}
+    for block in range(BLOCKS):
+        for side in range(2):
+            start = [jnp.zeros((8, LANES), jnp.float32)] * 3 + [jnp.ones((8, LANES), jnp.float32)]
+            sums[side, block] = walk(side, block, COLUMNS // 2 - 1, 0, start)
     for copy in speed_y:
         copy.wait_recv()
-    for key in sums:
-        sums[key] = ray(0, key[0], key[1], sums[key])
+    for side, place in enumerate((before_place, after_place)):
+        for block in range(BLOCKS):
+            value = speed_arrived[side, pl.ds(8 * block, 8)]
+            rows = pl.ds(TOP + 8 * block, 8)
+            speed[0, place, rows] = value
+            speed[1, place, rows] = pltpu.roll(value, NZ, 1)
+        for block in range(BLOCKS // 2):
+            value = speed_arrived[side, pl.ds(PLANES + 8 * block, 8)]
+            speed[2, place, pl.ds(TOP + 8 * block, 8)] = value
+            speed[2, place, pl.ds(TOP + PLANES // 2 + 8 * block, 8)] = pltpu.roll(value, NZ, 1)
+    for column in (0, COLUMNS - 1):
+        shade(column, everything)
+    for side, block in sums:
+        sums[side, block] = walk(side, block, 0, -1, sums[side, block])
 
     for block in range(BLOCKS):
         low, high = sums[0, block], sums[1, block]
@@ -658,9 +716,11 @@
             pltpu.VMEM((2, 2, 5, COLUMNS, LANES), jnp.float32),
             pltpu.VMEM((2, POPS, COLUMNS, LANES), jnp.float32),
             pltpu.VMEM((2, 5, COLUMNS, LANES), jnp.float32),
-            pltpu.VMEM((3, 2, 3, PLANES, LANES), jnp.float32),
-            pltpu.VMEM((3, 2, 3, PLANES, LANES), jnp.float32),
-            pltpu.VMEM((3, PLANES, LANES), jnp.float32),
+            pltpu.VMEM((3, 2, RIM_ROWS, LANES), jnp.float32),
+            pltpu.VMEM((3, 2, RIM_ROWS, LANES), jnp.float32),
+            pltpu.VMEM((2, SPEED_ROWS, LANES), jnp.float32),
+            pltpu.VMEM((2, SPEED_ROWS, LANES), jnp.float32),
+            pltpu.VMEM((4, COLUMNS, PLANES, LANES), jnp.float32),
             pltpu.VMEM((8, 16, LANES), jnp.float32),
             pltpu.VMEM((8, 16, LANES), jnp.float32),
             pltpu.VMEM((spans, 2, 16, LANES), jnp.float32),

time: 35.4 us -> 35 us (0.989)
  Pallas kernels: 34 us -> 33.6 us
where the time goes in v1:
time: 35 us; the launch traced here: 34.9 us
  Pallas kernels  33.6 us (96%)
  between operations  1.28 us (4%)
    pallas_call x1, Pallas kernels, on_device(): pl.pallas_call(functools.partial(kernel, spans, streams), out_shape=(jax....  31.2 us
    pallas_call x1, Pallas kernels, on_device(): pl.pallas_call(store_kernel, out_shape=(jax.ShapeDtypeStruct(final.shape,...  2.42 us

profile of v1, /device:TPU:0, one launch (start us, length us, event | category | flops | bytes accessed | tf_op | source)
XLA Modules:
  0.0 34.9 jit_solution(9596240102650898963)
XLA Ops:
  1.3 31.2 %shard_map.59 = (f32[19,32,2048]{2,1,0:T(8,128)S(1)}, f32[2,4,256]{2,1,0:T(4,128)S(1)}) custom-call(f32[19,32,2048]{2,1,0:T(8,128)} %populations.1, s32[1]{0:T(128)S(6)} %copy.6.camera_in, s32[32]{0:T(128)} %bitcast.2, s32[8]{0:T(128)} %bitcast.3), custom_call_target="tpu_custom_call" | custom-call | tf_op jit(solution)/shard_map/pallas_call | solution.py:699
  32.5 2.4 %shard_map.60 = (f32[19,32,2048]{2,1,0:T(8,128)}, f32[2,4,256]{2,1,0:T(4,128)}) custom-call(f32[19,32,2048]{2,1,0:T(8,128)S(1)} %get-tuple-element.4.final, f32[2,4,256]{2,1,0:T(4,128)S(1)} %get-tuple-element.5.tile_image), custom_call_target="tpu_custom_call" | custom-call | tf_op jit(solution)/shard_map/pallas_call | solution.py:737

commit v2 on v1

--- a/solution.py
+++ b/solution.py
@@ -465,7 +465,7 @@
     seam = (stream == 0).astype(jnp.int32)
     sweep(first_work, 0, COLUMNS, 4, everything, 0, 4 * seam)
     pl.semaphore_wait(barrier, len(partners))
-    send(x_sides[0] + corners[0] + y_sides[0])
+    send(corners[0] + x_sides[0] + y_sides[0])
     sweep(first_work, 0, COLUMNS, 4, everything, 4 * seam)
 
     for phase in (1, 2):
@@ -480,10 +480,10 @@
         inner(step_work)
         await_rims(phase - 1)
         post_strips(strip_values, edge_planes, store_edges(phase) if phase == 1 else store_deep)
-        send(x_sides[phase] + corners[phase])
+        send(corners[phase] + x_sides[phase])
         if phase == 2:
             post_strips(strip_values, second_planes, store_second)
-            send(late)
+            send(late[4:] + late[:4])
         post_rims(phase, lambda block: streamed(rim_reader(source, block)))
         send(y_sides[phase])
         outer(step_work)
@@ -640,7 +640,7 @@
     for number in range(8):
         outgoing[number] = foot[tile_order[number]]
     tiles = []
-    for hop, target in enumerate((span_up, span_down, span_far)):
+    for hop, target in enumerate((span_far, span_up, span_down)):
         tiles.append(
             remote(
                 outgoing.at[pl.ds(2 * target, 2)], incoming.at[span], TILE_BASE + hop, (stream, target)

time: 35 us -> 34.9 us (level)
  no operation moved by 1% of the time
where the time goes in v2:
time: 34.9 us; the launch traced here: 34.8 us
  Pallas kernels  33.5 us (96%)
  between operations  1.28 us (4%)
    pallas_call x1, Pallas kernels, on_device(): pl.pallas_call(functools.partial(kernel, spans, streams), out_shape=(jax....  31.1 us
    pallas_call x1, Pallas kernels, on_device(): pl.pallas_call(store_kernel, out_shape=(jax.ShapeDtypeStruct(final.shape,...  2.42 us

profile of v2, /device:TPU:0, one launch (start us, length us, event | category | flops | bytes accessed | tf_op | source)
XLA Modules:
  0.0 34.8 jit_solution(11286021340798562624)
XLA Ops:
  1.3 31.1 %shard_map.59 = (f32[19,32,2048]{2,1,0:T(8,128)S(1)}, f32[2,4,256]{2,1,0:T(4,128)S(1)}) custom-call(f32[19,32,2048]{2,1,0:T(8,128)} %populations.1, s32[1]{0:T(128)S(6)} %copy.6.camera_in, s32[32]{0:T(128)} %bitcast.2, s32[8]{0:T(128)} %bitcast.3), custom_call_target="tpu_custom_call" | custom-call | tf_op jit(solution)/shard_map/pallas_call | solution.py:699
  32.4 2.4 %shard_map.60 = (f32[19,32,2048]{2,1,0:T(8,128)}, f32[2,4,256]{2,1,0:T(4,128)}) custom-call(f32[19,32,2048]{2,1,0:T(8,128)S(1)} %get-tuple-element.4.final, f32[2,4,256]{2,1,0:T(4,128)S(1)} %get-tuple-element.5.tile_image), custom_call_target="tpu_custom_call" | custom-call | tf_op jit(solution)/shard_map/pallas_call | solution.py:737
